TPU v7x, 32 devices: a whole 2x2x4 slice. The times are simulated.
32 devices in a mesh: groups: 2 (over y), row: 4 (over z), col: 4 (over x, core).
Axes of the slice: x: 2, y: 2, z: 4, core: 2. Of those that a mesh axis runs over, the one named last changes fastest.
Arguments:
- activations: bfloat16 [1024, 8192], P(('groups', 'row'), 'col'), parts along dimension 0, may hold values from -6 to 6
- w_gate: bfloat16 [8192, 14336], P('row', 'col'), may hold values from -0.0625 to 0.0625
- w_up: bfloat16 [8192, 14336], P('row', 'col'), may hold values from -0.0625 to 0.0625
- w_down: bfloat16 [8192, 14336], P('row', 'col'), may hold values from -0.1875 to 0.1875
- block_lists: int32 [4, 4, 2], P('groups'), parts along dimension 0, may hold values from 0 to 28, as said below
Outputs:
- ffn_output: bfloat16 [1024, 8192], P(('groups', 'row'), 'col'), parts along dimension 0
There are 2 independent parts, one for each index of `groups`. A program takes and returns all parts, laid end to end along the dimension named above; an argument that names none is the same for every part. Nothing has to cross between parts.
Inputs may be any that keep to these rules, and one draw needn't show every extreme that they name: block_lists[b, c, 0] is a block of slab c; block_lists[b, c, 1] is another block of the same slab, or S = 14336 // (128 * 4) meaning none; some token block uses both entries of some slab.
All inputs are finite; a program needn't handle non-finite values.
Results may differ from a plain program's by a relative error of at most 0.011.
Values may be sent and summed in bfloat16 or wider, within the bound.
A program may use at most 192 MiB of HBM per device.

v0:
```python
import jax
import jax.numpy as jnp
from jax import lax
from jax.sharding import PartitionSpec as P


def partner_2(block, axis, stride):
    count = lax.axis_size(axis)
    route = []
    for low in range(count):
        high = low | 1 << stride
        if high != low and high < count:
            route += [(low, high), (high, low)]
    return lax.ppermute(block, axis, route)


def shards(activations, w_gate, w_up, w_down, block_lists):
    block_width = 128
    row_count = lax.axis_size("row")
    row_id = lax.axis_index("row")
    col_id = lax.axis_index("col")
    slab_blocks = w_gate.shape[1] // block_width
    gathered = lax.all_gather(activations, "col", axis=1, tiled=True)
    partner = partner_2(gathered, "row", 0)
    wanted = lax.dynamic_index_in_dim(block_lists, col_id, axis=1, keepdims=False).reshape(
        row_count
    )
    chosen = jnp.minimum(wanted, slab_blocks - 1)
    own_entry = lax.dynamic_index_in_dim(wanted, row_id, axis=0, keepdims=False)
    live_flag = (own_entry < slab_blocks).astype(jnp.float32)

    def outgoing(weight):
        pieces = weight.reshape(weight.shape[0], slab_blocks, block_width)
        return jnp.take(pieces, chosen, axis=1)

    def columns(received):
        return received.reshape(received.shape[0], block_width)

    got_gate, got_up, got_down = (
        lax.all_to_all(outgoing(w_gate), "row", split_axis=1, concat_axis=0, tiled=True),
        lax.all_to_all(outgoing(w_up), "row", split_axis=1, concat_axis=0, tiled=True),
        lax.all_to_all(outgoing(w_down), "row", split_axis=1, concat_axis=0, tiled=True),
    )
    gate_cols = columns(got_gate)
    up_cols = columns(got_up)

    def hidden_of(token_rows):
        gate_value = jnp.dot(token_rows, gate_cols, preferred_element_type=jnp.float32)
        up_value = jnp.dot(token_rows, up_cols, preferred_element_type=jnp.float32)
        return (jax.nn.relu(gate_value) * up_value * live_flag).astype(jnp.bfloat16)

    hidden_own = hidden_of(gathered)
    hidden_other = hidden_of(partner)
    down_cols = columns(got_down)
    own_partial = lax.dot_general(
        hidden_own, down_cols, (((1,), (1,)), ((), ())), preferred_element_type=jnp.float32
    )
    other_partial = lax.dot_general(
        hidden_other, down_cols, (((1,), (1,)), ((), ())), preferred_element_type=jnp.float32
    )
    own_rounded = own_partial.astype(jnp.bfloat16)
    other_rounded = other_partial.astype(jnp.bfloat16)
    received = partner_2(other_rounded, "row", 0)
    own_sum, other_sum = (
        lax.psum_scatter(
            own_rounded.astype(jnp.float32).astype(jnp.bfloat16),
            "col",
            scatter_dimension=1,
            tiled=True,
        ).astype(jnp.float32),
        lax.psum_scatter(
            received.astype(jnp.float32).astype(jnp.bfloat16),
            "col",
            scatter_dimension=1,
            tiled=True,
        ).astype(jnp.float32),
    )
    result = own_sum + other_sum
    return result.astype(jnp.bfloat16)


def solution(mesh):
    in_specs = (
        P(("groups", "row"), "col"),
        P("row", "col"),
        P("row", "col"),
        P("row", "col"),
        P("groups", None, None),
    )
    out_specs = P(("groups", "row"), "col")
    return jax.shard_map(shards, mesh=mesh, in_specs=in_specs, out_specs=out_specs, check_vma=False)
```

profile of v0, /device:TPU:1, one launch (start us, length us, event | category | flops | bytes accessed | tf_op | source)
XLA Modules:
  0.0 439.0 jit_solution(7371598521434588314)
XLA Ops:
  6.5 0.0 copy-start
  6.5 20.2 %copy.6 = bf16[2048,3584]{0,1:T(8,128)(2,1)} copy(bf16[2048,3584]{1,0:T(8,128)(2,1)} %param.8) | data formatting | bytes 29360128 | tf_op args[1]
  26.7 20.3 %copy.7 = bf16[2048,28,128]{2,0,1:T(8,128)(2,1)} copy(bf16[2048,28,128]{0,2,1:T(8,128)(2,1)} %bitcast.35) | data formatting | bytes 29360128 | tf_op jit(solution)/shard_map/reshape | solution.py:33
  47.0 0.0 copy-done
  47.0 0.2 dynamic-slice_reduce_fusion
  47.2 0.1 reshape.35
  47.3 19.0 %copy.8 = bf16[2048,3584]{0,1:T(8,128)(2,1)} copy(bf16[2048,3584]{1,0:T(8,128)(2,1)} %param.9) | data formatting | bytes 29360128 | tf_op args[2]
  66.3 20.3 %copy.9 = bf16[2048,28,128]{2,0,1:T(8,128)(2,1)} copy(bf16[2048,28,128]{0,2,1:T(8,128)(2,1)} %bitcast.36) | data formatting | bytes 29360128 | tf_op jit(solution)/shard_map/reshape | solution.py:33
  86.6 6.1 %gather_fusion = bf16[4,2048,128]{2,1,0:T(8,128)(2,1)S(1)} fusion(bf16[2048,28,128]{2,0,1:T(8,128)(2,1)} %copy.7, s32[1024]{0:T(1024)S(1)} %pad_clamp_fusion), kind=kCustom, calls=%fused_computation.clone | custom fusion | bytes 4194320 | tf_op jit(solution)/shard_map/jit(_take)/gather | solution.py:34
  92.7 7.3 %gather_fusion.1 = bf16[4,2048,128]{2,1,0:T(8,128)(2,1)} fusion(bf16[2048,28,128]{2,0,1:T(8,128)(2,1)} %copy.9, s32[1024]{0:T(1024)S(1)} %pad_clamp_fusion), kind=kCustom, calls=%fused_computation.1.clone | custom fusion | bytes 4194320 | tf_op jit(solution)/shard_map/jit(_take)/gather | solution.py:34
  100.0 20.1 %copy.10 = bf16[2048,3584]{0,1:T(8,128)(2,1)} copy(bf16[2048,3584]{1,0:T(8,128)(2,1)} %param.10) | data formatting | bytes 29360128 | tf_op args[3]
  120.2 20.3 %copy.11 = bf16[2048,28,128]{2,0,1:T(8,128)(2,1)} copy(bf16[2048,28,128]{0,2,1:T(8,128)(2,1)} %bitcast.37) | data formatting | bytes 29360128 | tf_op jit(solution)/shard_map/reshape | solution.py:33
  140.4 7.3 %gather_fusion.2 = bf16[4,2048,128]{2,1,0:T(8,128)(2,1)} fusion(bf16[2048,28,128]{2,0,1:T(8,128)(2,1)} %copy.11, s32[1024]{0:T(1024)S(1)} %pad_clamp_fusion), kind=kCustom, calls=%fused_computation.2.clone | custom fusion | bytes 4194320 | tf_op jit(solution)/shard_map/jit(_take)/gather | solution.py:34
  147.7 4.9 %select_bitcast_fusion.2 = (bf16[2048,4,128]{2,0,1:T(8,128)(2,1)}, bf16[2048,4,128]{2,0,1:T(8,128)(2,1)}, bf16[2048,4,128]{2,0,1:T(8,128)(2,1)S(1)}) fusion(bf16[4,2048,128]{2,1,0:T(8,128)(2,1)S(1)} %gather_fusion, pred[4]{0:T(512)(128)(4,1)S(1)} %get-tuple-element.6, bf16[4,2048,128]{2,1,0:T(8,128)(2,1)} %gather_fusion.1, bf16[4,2048,128]{2,1,0:T(8,128)(2,1)} %gather_fusion.2), kind=kLoop, calls=%fused_computation.7 | loop fusion | flops 3145728 | bytes 12582916 | tf_op jit(solution)/shard_map/jit(_take)/select_n | solution.py:34
  152.6 52.7 %all_to_all.45 = bf16[2048,4,128]{2,0,1:T(8,128)(2,1)} all-to-all(bf16[2048,4,128]{2,0,1:T(8,128)(2,1)S(1)} %get-tuple-element.10), channel_id=1, replica_groups=mesh['groups'=2,'row'=4,'col'=4] {'row'}, dimensions={1} | all-to-all | bytes 4194304 | tf_op jit(solution)/shard_map/all_to_all | solution.py:42
  205.3 3.6 all-to-all-start
  208.9 0.0 all-gather.2.cloned.1.call-start
  208.9 0.7 all-gather.2.cloned.1.call-update
  209.6 46.9 %all-to-all-done = bf16[2048,4,128]{2,0,1:T(8,128)(2,1)S(1)} async-done(((bf16[2048,4,128]{2,0,1:T(8,128)(2,1)}), bf16[2048,4,128]{2,0,1:T(8,128)(2,1)S(1)}, u32[]{:S(2)}, u32[]{:S(2)}) %all-to-all-start) | async-done | bytes 2097184 | tf_op jit(solution)/shard_map/all_to_all | solution.py:40
  256.5 4.5 %all-to-all-start.1 = ((bf16[2048,4,128]{2,0,1:T(8,128)(2,1)}), bf16[2048,4,128]{2,0,1:T(8,128)(2,1)}, u32[]{:S(2)}, u32[]{:S(2)}) async-start(bf16[2048,4,128]{2,0,1:T(8,128)(2,1)} %get-tuple-element.9), calls=%async_computation.1 | async-start | bytes 4194304 | tf_op jit(solution)/shard_map/all_to_all | solution.py:41
  261.0 0.0 reduce-scatter.3.cloned.1.call-start
  261.1 0.6 dynamic_slice.9
  262.3 0.0 all-gather.2.cloned.1.call-done
  262.3 1.4 collective-permute-start
  263.8 2.4 convolution_maximum_fusion.1
  266.2 42.6 %all-to-all-done.1 = bf16[2048,4,128]{2,0,1:T(8,128)(2,1)} async-done(((bf16[2048,4,128]{2,0,1:T(8,128)(2,1)}), bf16[2048,4,128]{2,0,1:T(8,128)(2,1)}, u32[]{:S(2)}, u32[]{:S(2)}) %all-to-all-start.1) | async-done | bytes 2097184 | tf_op jit(solution)/shard_map/all_to_all | solution.py:41
  308.8 6.7 %convolution_convert_fusion.1 = bf16[128,8192]{1,0:T(8,128)(2,1)} fusion(bf16[8192,128]{1,0:T(8,128)(2,1)} %bitcast.40, f32[128,128]{1,0:T(8,128)S(1)} %convolution_maximum_fusion.1, bf16[8192,128]{1,0:T(8,128)(2,1)} %bitcast.9, bf16[128,8192]{1,0:T(8,128)(2,1)} %all-gather.2.cloned.1.call-done, f32[]{:T(128)} %bitcast.10), kind=kOutput, calls=%fused_computation.4 | convolution fusion | flops 537968640 | bytes 8454148 | tf_op jit(solution)/shard_map/dot_general | solution.py:55
  315.5 0.0 reduce-scatter.3.cloned.1.call-update
  315.5 0.0 reduce-scatter.5.cloned.1.call-start
  315.5 25.1 %collective-permute-done = bf16[128,8192]{1,0:T(8,128)(2,1)} collective-permute-done((bf16[128,8192]{1,0:T(8,128)(2,1)}, bf16[128,8192]{1,0:T(8,128)(2,1)}, u32[]{:S(2)}, u32[]{:S(2)}) %collective-permute-start) | collective-permute-done | bytes 2097184 | tf_op jit(solution)/shard_map/ppermute | solution.py:14
  340.7 3.0 fusion.9
  343.7 0.0 copy-start.1
  343.7 6.1 %convolution_convert_fusion = bf16[128,8192]{1,0:T(8,128)(2,1)} fusion(bf16[8192,128]{1,0:T(8,128)(2,1)} %bitcast.41, f32[128,128]{1,0:T(8,128)S(1)} %fusion.9, bf16[8192,128]{1,0:T(8,128)(2,1)S(1)} %bitcast.39, bf16[128,8192]{1,0:T(8,128)(2,1)} %collective-permute-done, f32[]{:T(128)} %bitcast.10), kind=kOutput, calls=%fused_computation.3 | convolution fusion | flops 537985024 | bytes 8454148 | tf_op jit(solution)/shard_map/dot_general | solution.py:58
  349.8 0.3 collective-permute-start.1
  350.1 44.7 %collective-permute-done.1 = bf16[128,8192]{1,0:T(8,128)(2,1)S(1)} collective-permute-done((bf16[128,8192]{1,0:T(8,128)(2,1)}, bf16[128,8192]{1,0:T(8,128)(2,1)S(1)}, u32[]{:S(2)}, u32[]{:S(2)}) %collective-permute-start.1) | collective-permute-done | bytes 2097184 | tf_op jit(solution)/shard_map/ppermute | solution.py:14
  394.8 0.0 copy-start.2
  394.8 1.3 copy-done.2
  396.1 0.0 reduce-scatter.5.cloned.1.call-update
  396.2 0.0 reduce-scatter.3.cloned.1.call-done
  396.2 34.2 %reduce-scatter.5.cloned.1.call-done = bf16[128,2048]{1,0:T(8,128)(2,1)} async-done(((bf16[128,8192]{1,0:T(8,128)(2,1)}), bf16[128,2048]{1,0:T(8,128)(2,1)}) %reduce-scatter.5.cloned.1.call-update) | async-done | bytes 524304 | tf_op jit(solution)/shard_map/reduce_scatter | solution.py:71
  430.4 2.1 add_convert_fusion
  432.5 0.0 copy-done.1
  (2 shorter events, 0.0 us)
Async XLA Ops:
  6.5 40.4 %copy-start = (s32[2,4,2]{1,2,0:T(2,128)S(1)}, s32[2,4,2]{1,2,0:T(2,128)}, u32[]{:S(2)}) copy-start(s32[2,4,2]{1,2,0:T(2,128)} %param.11) | copy-start | bytes 196
  205.3 51.3 %all-to-all-start = ((bf16[2048,4,128]{2,0,1:T(8,128)(2,1)}), bf16[2048,4,128]{2,0,1:T(8,128)(2,1)S(1)}, u32[]{:S(2)}, u32[]{:S(2)}) async-start(bf16[2048,4,128]{2,0,1:T(8,128)(2,1)} %get-tuple-element.8), calls=%async_computation | async-start | bytes 4194304 | tf_op jit(solution)/shard_map/all_to_all | solution.py:40
  208.9 53.4 %all-gather.2.cloned.1.call-start = ((), (), s32[]{:S(2)}) async-start(), calls=%async_computation.5 | async-start | bytes 2621440 | tf_op jit(solution)/shard_map/all_gather | solution.py:23
  256.5 52.3 %all-to-all-start.1 = ((bf16[2048,4,128]{2,0,1:T(8,128)(2,1)}), bf16[2048,4,128]{2,0,1:T(8,128)(2,1)}, u32[]{:S(2)}, u32[]{:S(2)}) async-start(bf16[2048,4,128]{2,0,1:T(8,128)(2,1)} %get-tuple-element.9), calls=%async_computation.1 | async-start | bytes 4194304 | tf_op jit(solution)/shard_map/all_to_all | solution.py:41
  261.0 135.2 %reduce-scatter.3.cloned.1.call-start = ((), (), s32[]{:S(2)}) async-start(), calls=%async_computation.6 | async-start | bytes 2621440 | tf_op jit(solution)/shard_map/reduce_scatter | solution.py:65
  262.3 78.3 %collective-permute-start = (bf16[128,8192]{1,0:T(8,128)(2,1)}, bf16[128,8192]{1,0:T(8,128)(2,1)}, u32[]{:S(2)}, u32[]{:S(2)}) collective-permute-start(bf16[128,8192]{1,0:T(8,128)(2,1)} %all-gather.2.cloned.1.call-done), channel_id=1, source_target_pairs={{0,4},{4,0},{8,12},{12,8},{1,5},{5,1},{9,13},{13,9},{2,6},{6,2},{1... | collective-permute-start | bytes 6291464 | tf_op jit(solution)/shard_map/ppermute | solution.py:14
  315.5 114.9 %reduce-scatter.5.cloned.1.call-start = ((), (), s32[]{:S(2)}) async-start(), calls=%async_computation.7 | async-start | bytes 2621440 | tf_op jit(solution)/shard_map/reduce_scatter | solution.py:71
  343.7 88.8 %copy-start.1 = (s32[2,4,2]{1,2,0:T(2,128)S(1)}, s32[2,4,2]{1,2,0:T(2,128)}, u32[]{:S(2)}) copy-start(s32[2,4,2]{1,2,0:T(2,128)} %param.11) | copy-start | bytes 196
  349.8 45.0 %collective-permute-start.1 = (bf16[128,8192]{1,0:T(8,128)(2,1)}, bf16[128,8192]{1,0:T(8,128)(2,1)S(1)}, u32[]{:S(2)}, u32[]{:S(2)}) collective-permute-start(bf16[128,8192]{1,0:T(8,128)(2,1)} %convolution_convert_fusion), channel_id=1, source_target_pairs={{0,4},{4,0},{8,12},{12,8},{1,5},{5,1},{9,13},{13,9},{2,6},{6,2},{1... | collective-permute-start | bytes 6291464 | tf_op jit(solution)/shard_map/ppermute | solution.py:14
  394.8 1.3 copy-start.2
Sparse Core Ops, SparseCore 0:
  211.3 25.5 all-gather.1
  315.6 31.3 reduce-scatter.2
  396.3 34.0 reduce-scatter.4
where the time goes:
time: 443 us; the launch traced here: 439 us
  waiting for transfers between devices  194 us (44%)
  local copies, waits for them, and re-layouts  143 us (32%)
  blocking collectives  52.7 us (12%)
  matrix products  18.2 us (4%)
  between operations  13.9 us (3%)
  starting transfers between devices  9.96 us (2%)
  other arithmetic  7.02 us (2%)
    ppermute x2, waiting for transfers between devices, partner_2(): return lax.ppermute(block, axis, route)  69.8 us
    reshape x3, local copies, waits for them, and re-layouts, outgoing(): pieces = weight.reshape(weight.shape[0], slab_blocks, block_width)  60.8 us
    unnamed x9, local copies, waits for them, and re-layouts  60.6 us
    all_to_all x1, blocking collectives, shards(): lax.all_to_all(outgoing(w_down), 'row', split_axis=1, concat_axis=0, tile...  52.7 us
    all_to_all x1, waiting for transfers between devices, shards(): lax.all_to_all(outgoing(w_gate), 'row', split_axis=1, concat_axis=0, tile...  46.9 us
    all_to_all x1, waiting for transfers between devices, shards(): lax.all_to_all(outgoing(w_up), 'row', split_axis=1, concat_axis=0, tiled=...  42.6 us
    reduce_scatter x1, waiting for transfers between devices, shards(): lax.psum_scatter(received.astype(jnp.float32).astype(jnp.bfloat16), 'col'...  34.2 us
    gather x3, local copies, waits for them, and re-layouts, outgoing(): return jnp.take(pieces, chosen, axis=1)  20.7 us
  transfers between devices with their start and end apart: 7, of which 5 were waited for; matrix products, arithmetic and copies ran while one was open for 4% of the time, Pallas kernels for 0%

commit v1 on v0

v1 whole, which is shorter than its diff:
```python
import functools

import jax
import jax.numpy as jnp
from jax import lax
from jax.experimental import pallas as pl
from jax.experimental.pallas import tpu as pltpu
from jax.sharding import PartitionSpec as P

WIDTH = 128
PARTS = 2


def partner_2(block, axis, stride):
    count = lax.axis_size(axis)
    route = []
    for low in range(count):
        high = low | 1 << stride
        if high != low and high < count:
            route += [(low, high), (high, low)]
    return lax.ppermute(block, axis, route)


def general_shards(activations, w_gate, w_up, w_down, block_lists):
    row_count = lax.axis_size("row")
    row_id = lax.axis_index("row")
    col_id = lax.axis_index("col")
    slab_blocks = w_gate.shape[1] // WIDTH
    gathered = lax.all_gather(activations, "col", axis=1, tiled=True)
    partner = partner_2(gathered, "row", 0)
    wanted = lax.dynamic_index_in_dim(block_lists, col_id, axis=1, keepdims=False).reshape(
        row_count
    )
    chosen = jnp.minimum(wanted, slab_blocks - 1)
    own_entry = lax.dynamic_index_in_dim(wanted, row_id, axis=0, keepdims=False)
    live_flag = (own_entry < slab_blocks).astype(jnp.float32)

    def fetch(weight):
        pieces = weight.reshape(weight.shape[0], slab_blocks, WIDTH)
        outgoing = jnp.take(pieces, chosen, axis=1)
        got = lax.all_to_all(outgoing, "row", split_axis=1, concat_axis=0, tiled=True)
        return got.reshape(got.shape[0], WIDTH)

    gate_cols, up_cols, down_cols = fetch(w_gate), fetch(w_up), fetch(w_down)

    def term_of(token_rows):
        gate_value = jnp.dot(token_rows, gate_cols, preferred_element_type=jnp.float32)
        up_value = jnp.dot(token_rows, up_cols, preferred_element_type=jnp.float32)
        hidden = (jax.nn.relu(gate_value) * up_value * live_flag).astype(jnp.bfloat16)
        return lax.dot_general(
            hidden, down_cols, (((1,), (1,)), ((), ())), preferred_element_type=jnp.float32
        ).astype(jnp.bfloat16)

    own = term_of(gathered)
    received = partner_2(term_of(partner), "row", 0)
    own_sum, other_sum = (
        lax.psum_scatter(term, "col", scatter_dimension=1, tiled=True).astype(jnp.float32)
        for term in (own, received)
    )
    return (own_sum + other_sum).astype(jnp.bfloat16)


def pick_kernel(lists, col, gate, up, down, gate_out, up_out, down_out):
    gate_out[0] = gate[...]
    up_out[0] = up[...]
    down_out[0] = down[...]


def pick(block_lists, col_id, w_gate, w_up, w_down):
    depth, slab = w_gate.shape
    blocks = block_lists.shape[0]
    top = slab // WIDTH - 1

    def chosen(b, s, lists, col):
        return 0, jnp.minimum(lists[b, col[0], s], top)

    shape = jax.ShapeDtypeStruct((blocks, depth, 2 * WIDTH), w_gate.dtype)
    return pl.pallas_call(
        pick_kernel,
        grid_spec=pltpu.PrefetchScalarGridSpec(
            num_scalar_prefetch=2,
            grid=(blocks, 2),
            in_specs=[pl.BlockSpec((depth, WIDTH), chosen)] * 3,
            out_specs=[pl.BlockSpec((1, depth, WIDTH), lambda b, s, lists, col: (b, 0, s))] * 3,
        ),
        out_shape=[shape] * 3,
        compiler_params=pltpu.CompilerParams(vmem_limit_bytes=32 * 2**20),
    )(block_lists, col_id, w_gate, w_up, w_down)


def layer_kernel(
    slab_blocks, lists, act, w_gate, w_up, w_down, out,
    gate_w, up_w, down_w, x_all, part_f32, part_out, part_in, hid_all,
    term, term_in, half_out, half_in, sum_out,
    w_sem, a_send, a_recv, g1_send, g1_recv, g2_send, g2_recv, g3_send, g3_recv,
    p_send, p_recv, h_send, h_recv, t_send, t_recv, s_send, s_recv, o_send, o_recv,
):
    parts, rows, cols, size, depth = x_all.shape
    blocks = rows // 2
    toks = cols * size
    r, c = lax.axis_index("row"), lax.axis_index("col")
    core, chip = c % 2, c // 2
    c1 = c + 1 - 2 * core
    c2 = (c + 2) % 4
    c3 = (c1 + 2) % 4

    loads = [
        pltpu.make_async_copy(w_gate, gate_w, w_sem.at[0]),
        pltpu.make_async_copy(w_up, up_w, w_sem.at[1]),
        pltpu.make_async_copy(w_down, down_w, w_sem.at[2]),
    ]
    for load in loads:
        load.start()

    barrier = pltpu.get_barrier_semaphore()
    for dr in range(rows):
        for dc in range(cols):
            if dr or dc:
                pl.semaphore_signal(
                    barrier, inc=1,
                    device_id={"row": (r + dr) % rows, "col": (c + dc) % cols},
                    device_id_type=pl.DeviceIdType.MESH,
                )
    pl.semaphore_wait(barrier, rows * cols - 1)

    drains = []

    def remote(src, dst, send, recv, row, col):
        return pltpu.make_async_remote_copy(
            src_ref=src, dst_ref=dst, send_sem=send, recv_sem=recv,
            device_id={"row": row, "col": col}, device_id_type=pl.DeviceIdType.MESH,
        )

    def send_to(src, dst, send, recv, row, col):
        copy = remote(src, dst, send, recv, row, col)
        copy.start()
        drains.append((None, copy))

    def send_or_keep(src, dst, send, recv, row, col):
        other = jnp.logical_or(row != r, col != c)
        copy = remote(src, dst, send, recv, row, col)

        @pl.when(other)
        def _():
            copy.start()

        @pl.when(jnp.logical_not(other))
        def _():
            pltpu.make_async_copy(src, dst, recv).start()

        drains.append((other, copy))

    def arrived(dst, recv):
        pltpu.make_async_copy(dst, dst, recv).wait()

    def spread(p):
        for q in range(cols):
            send_or_keep(
                act.at[pl.ds((p * cols + q) * size, size)], x_all.at[p, r, q],
                a_send.at[p, q], a_recv.at[p, r], c, q,
            )

    def forward(p):
        for k in range(rows):
            s = (r + k) % rows
            piece = x_all.at[p, s, c]
            arrived(piece, a_recv.at[p, s])
            send_to(piece, piece, g2_send.at[p, k], g2_recv.at[p, s], r, c2)
            send_to(piece, piece, g1_send.at[p, k], g1_recv.at[p, s], r, c1)

    def forward_again(p):
        for k in range(rows):
            s = (r + k) % rows
            piece = x_all.at[p, s, c2]
            arrived(piece, g2_recv.at[p, s])
            send_to(piece, piece, g3_send.at[p, k], g3_recv.at[p, s], r, c1)

    def collected(p):
        for s in range(rows):
            arrived(x_all.at[p, s, c1], g1_recv.at[p, s])
        for s in range(rows):
            arrived(x_all.at[p, s, c3], g3_recv.at[p, s])

    def gate_up(p):
        for b in range(blocks):
            x = x_all[p, 2 * b : 2 * b + 2].reshape(2 * toks, depth)
            for j, weight in enumerate((gate_w, up_w)):
                value = jnp.dot(x, weight[b], preferred_element_type=jnp.float32)
                value = value.reshape(2, toks, 2 * WIDTH)
                lanes = slice(j * 2 * WIDTH, (j + 1) * 2 * WIDTH)
                part_f32[p, 2 * b : 2 * b + 2, :, lanes] = value
                part_out[p, 2 * b : 2 * b + 2, :, lanes] = value.astype(jnp.bfloat16)
        for k in range(1, rows):
            s = (r + k) % rows
            send_to(part_out.at[p, s], part_in.at[p, k - 1], p_send.at[p, k], p_recv.at[p, k], s, c)

    def hidden(p):
        total = part_f32[p, r]
        for k in range(1, rows):
            arrived(part_in.at[p, k - 1], p_recv.at[p, k])
            total = total + part_in[p, k - 1].astype(jnp.float32)
        value = jnp.maximum(total[:, : 2 * WIDTH], 0.0) * total[:, 2 * WIDTH :]
        live = [jnp.where(lists[r // 2, c, s] < slab_blocks, 1.0, 0.0) for s in range(2)]
        lane = lax.broadcasted_iota(jnp.int32, value.shape, 1)
        value = value * jnp.where(lane < WIDTH, live[0], live[1])
        hid_all[p, r] = value.astype(jnp.bfloat16)
        for k in range(1, rows):
            mine = hid_all.at[p, r]
            send_to(mine, mine, h_send.at[p, k], h_recv.at[p, k], (r + k) % rows, c)

    def down(p):
        for k in range(1, rows):
            arrived(hid_all.at[p, (r + rows - k) % rows], h_recv.at[p, k])
        tile = 512
        for b in range(blocks):
            h = hid_all[p, 2 * b : 2 * b + 2].reshape(2 * toks, 2 * WIDTH)
            for n in range(0, depth, tile):
                value = lax.dot_general(
                    h, down_w[b, n : n + tile], (((1,), (1,)), ((), ())),
                    preferred_element_type=jnp.float32,
                ).astype(jnp.bfloat16)
                for i in range(2):
                    for q in range(cols):
                        at = (i * cols + q) * size
                        term[p, q % 2, q // 2, 2 * b + i, :, n : n + tile] = value[at : at + size]
        send_to(term.at[p, 1 - core], term_in.at[p], t_send.at[p], t_recv.at[p], r, c1)

    def pair(p):
        arrived(term_in.at[p], t_recv.at[p])
        for k in range(rows):
            s = (r + k) % rows
            value = term[p, core, 1 - chip, s].astype(jnp.float32)
            value = value + term_in[p, 1 - chip, s].astype(jnp.float32)
            half_out[p, s] = value.astype(jnp.bfloat16)
            send_to(half_out.at[p, s], half_in.at[p, s], s_send.at[p, k], s_recv.at[p, s], r, c2)

    def finish(p):
        for k in range(rows):
            s = (r + k) % rows
            value = term[p, core, chip, s].astype(jnp.float32)
            value = value + term_in[p, chip, s].astype(jnp.float32)
            arrived(half_in.at[p, s], s_recv.at[p, s])
            value = value + half_in[p, s].astype(jnp.float32)
            sum_out[p, s] = value.astype(jnp.bfloat16)
            send_or_keep(
                sum_out.at[p, s], out.at[pl.ds((p * cols + c) * size, size)],
                o_send.at[p, k], o_recv.at[p, c], s, r,
            )

    for p in range(parts):
        spread(p)
    forward(0)
    forward_again(0)
    forward(1)
    collected(0)
    loads[0].wait()
    loads[1].wait()
    gate_up(0)
    forward_again(1)
    collected(1)
    gate_up(1)
    hidden(0)
    loads[2].wait()
    down(0)
    hidden(1)
    pair(0)
    down(1)
    finish(0)
    pair(1)
    finish(1)
    for p in range(parts):
        for q in range(cols):
            arrived(out.at[pl.ds((p * cols + q) * size, size)], o_recv.at[p, q])
    for other, copy in drains:
        if other is None:
            copy.wait_send()
        else:
            pl.when(other)(copy.wait_send)


def layer(block_lists, activations, gate, up, down, rows, cols, slab_blocks):
    tokens, depth = activations.shape
    size = tokens // (PARTS * cols)
    toks = cols * size
    bf16, f32 = jnp.bfloat16, jnp.float32
    sem = pltpu.SemaphoreType.DMA
    by_row, by_col = sem((PARTS, rows)), sem((PARTS, cols))
    return pl.pallas_call(
        functools.partial(layer_kernel, slab_blocks),
        out_shape=jax.ShapeDtypeStruct(activations.shape, bf16),
        in_specs=[pl.BlockSpec(memory_space=pltpu.SMEM)] + [pl.BlockSpec(memory_space=pl.ANY)] * 4,
        out_specs=pl.BlockSpec(memory_space=pltpu.VMEM),
        scratch_shapes=[
            pltpu.VMEM(gate.shape, bf16),
            pltpu.VMEM(up.shape, bf16),
            pltpu.VMEM(down.shape, bf16),
            pltpu.VMEM((PARTS, rows, cols, size, depth), bf16),
            pltpu.VMEM((PARTS, rows, toks, 4 * WIDTH), f32),
            pltpu.VMEM((PARTS, rows, toks, 4 * WIDTH), bf16),
            pltpu.VMEM((PARTS, rows - 1, toks, 4 * WIDTH), bf16),
            pltpu.VMEM((PARTS, rows, toks, 2 * WIDTH), bf16),
            pltpu.VMEM((PARTS, 2, 2, rows, size, depth), bf16),
            pltpu.VMEM((PARTS, 2, rows, size, depth), bf16),
            pltpu.VMEM((PARTS, rows, size, depth), bf16),
            pltpu.VMEM((PARTS, rows, size, depth), bf16),
            pltpu.VMEM((PARTS, rows, size, depth), bf16),
            sem((3,)),
            by_col, by_row,
            by_row, by_row, by_row, by_row, by_row, by_row,
            by_row, by_row, by_row, by_row,
            sem((PARTS,)), sem((PARTS,)),
            by_row, by_row, by_row, by_col,
        ],
        compiler_params=pltpu.CompilerParams(
            collective_id=0, has_side_effects=True, vmem_limit_bytes=48 * 2**20
        ),
    )(block_lists, activations, gate, up, down)


def near_shards(rows, cols, activations, w_gate, w_up, w_down, block_lists):
    slab_blocks = w_gate.shape[1] // WIDTH
    col_id = lax.axis_index("col").astype(jnp.int32).reshape(1)
    gate, up, down = pick(block_lists, col_id, w_gate, w_up, w_down)
    return layer(block_lists, activations, gate, up, down, rows, cols, slab_blocks)


def solution(mesh):
    rows, cols = mesh.shape["row"], mesh.shape["col"]
    near = rows == 4 and cols == 4
    body = functools.partial(near_shards, rows, cols) if near else general_shards
    in_specs = (
        P(("groups", "row"), "col"),
        P("row", "col"),
        P("row", "col"),
        P("row", "col"),
        P("groups", None, None),
    )
    out_specs = P(("groups", "row"), "col")
    return jax.shard_map(body, mesh=mesh, in_specs=in_specs, out_specs=out_specs, check_vma=False)
```

time: 443 us -> 90 us (0.20)
  waiting for transfers between devices: 194 us -> 0 us
  local copies, waits for them, and re-layouts: 143 us -> 8.07 us
  Pallas kernels: 0 us -> 81.7 us
  blocking collectives: 52.7 us -> 0 us
  matrix products: 18.2 us -> 0 us
  between operations: 13.9 us -> 0.03 us
  starting transfers between devices: 9.96 us -> 0 us
  other arithmetic: 7.02 us -> 0 us
    all_to_all x2 -> x0, waiting for transfers between devices: 89.5 us -> none  [the longest x1 46.9 us: shards(): lax.all_to_all(outgoing(w_gate), 'row', split_axis=1, concat_axis=0, tile...]
    pallas_call x0 -> x2, Pallas kernels: none -> 81.7 us  [the longest x1 76.9 us: layer(): pl.pallas_call(functools.partial(layer_kernel, slab_blocks), out_shape=ja...]
    ppermute x2 -> x0, waiting for transfers between devices: 69.8 us -> none  [partner_2(): return lax.ppermute(block, axis, route)]
    reshape x4 -> x0, local copies, waits for them, and re-layouts: 60.9 us -> none  [the longest x3 60.8 us: outgoing(): pieces = weight.reshape(weight.shape[0], slab_blocks, block_width)]
    all_to_all x1 -> x0, blocking collectives: 52.7 us -> none  [shards(): lax.all_to_all(outgoing(w_down), 'row', split_axis=1, concat_axis=0, tile...]
    unnamed x9 -> x8, local copies, waits for them, and re-layouts: 60.6 us -> 8.07 us
    reduce_scatter x2 -> x0, waiting for transfers between devices: 34.2 us -> none  [the longest x1 34.2 us: shards(): lax.psum_scatter(received.astype(jnp.float32).astype(jnp.bfloat16), 'col'...]
    gather x3 -> x0, local copies, waits for them, and re-layouts: 20.7 us -> none  [outgoing(): return jnp.take(pieces, chosen, axis=1)]
  transfers between devices with their start and end apart: 7 -> 0, of which waited for: 5 -> 0; matrix products, arithmetic and copies ran while one was open for 4% -> 0% of each run, Pallas kernels for 0% -> 0%
where the time goes in v1:
time: 90 us; the launch traced here: 89.8 us
  Pallas kernels  81.7 us (91%)
  local copies, waits for them, and re-layouts  8.07 us (9%)
    pallas_call x1, Pallas kernels, layer(): pl.pallas_call(functools.partial(layer_kernel, slab_blocks), out_shape=ja...  76.9 us
    unnamed x8, local copies, waits for them, and re-layouts  8.07 us
    pallas_call x1, Pallas kernels, pick(): pl.pallas_call(pick_kernel, grid_spec=pltpu.PrefetchScalarGridSpec(num_sc...  4.73 us

profile of v1, /device:TPU:1, one launch (start us, length us, event | category | flops | bytes accessed | tf_op | source)
XLA Modules:
  0.0 89.8 jit_solution(11307804200886293805)
XLA Ops:
  0.0 0.8 copy.7.lists
  0.8 0.0 copy-start
  0.8 5.2 %copy-done = bf16[2048,3584]{1,0:T(8,128)(2,1)S(1)} copy-done((bf16[2048,3584]{1,0:T(8,128)(2,1)S(1)}, bf16[2048,3584]{1,0:T(8,128)(2,1)}, u32[]{:S(2)}) %copy-start) | copy-done | bytes 14680088
  5.9 0.0 copy-start.2
  5.9 4.7 %shard_map.55 = (bf16[2,2048,256]{2,1,0:T(8,128)(2,1)S(1)}, bf16[2,2048,256]{2,1,0:T(8,128)(2,1)S(1)}, bf16[2,2048,256]{2,1,0:T(8,128)(2,1)S(1)}) custom-call(s32[2,4,2]{2,1,0:T(4,128)S(1)} %copy.7.lists, s32[1]{0:T(128)} %bitcast.col, bf16[2048,3584]{1,0:T(8,128)(2,1)S(1)} %copy-done, bf16[2048,3584]{1,0:T(8,128)(2,1)} %up.1, bf16[2048,3584]{1,0:T(8,128)(2,1)} %down.1), custom_call_target="tpu_custom_call" | custom-call | tf_op jit(solution)/shard_map/pallas_call | solution.py:78
  10.7 0.0 copy-start.1
  10.7 1.3 %copy-done.1 = bf16[2,2048,256]{2,1,0:T(8,128)(2,1)} copy-done((bf16[2,2048,256]{2,1,0:T(8,128)(2,1)}, bf16[2,2048,256]{2,1,0:T(8,128)(2,1)S(1)}, u32[]{:S(2)}) %copy-start.1) | copy-done | bytes 2097176
  12.0 0.0 copy-done.2
  12.0 76.9 %shard_map.56 = bf16[128,2048]{1,0:T(8,128)(2,1)S(1)} custom-call(s32[2,4,2]{2,1,0:T(4,128)S(1)} %copy.7.lists, bf16[128,2048]{1,0:T(8,128)(2,1)S(1)} %copy-done.2, bf16[2,2048,256]{2,1,0:T(8,128)(2,1)S(1)} %get-tuple-element.8.w_gate, bf16[2,2048,256]{2,1,0:T(8,128)(2,1)S(1)} %get-tuple-element.9.w_up, bf16[2,2048,256]{2,1,0:T(8,128)(2,1)} %copy-done.1), custom_call_target="tpu_custom_call" | custom-call | tf_op jit(solution)/shard_map/pallas_call | solution.py:288
  89.0 0.8 copy.9
Async XLA Ops:
  0.8 5.2 %copy-start = (bf16[2048,3584]{1,0:T(8,128)(2,1)S(1)}, bf16[2048,3584]{1,0:T(8,128)(2,1)}, u32[]{:S(2)}) copy-start(bf16[2048,3584]{1,0:T(8,128)(2,1)} %gate.1) | copy-start | bytes 44040196
  5.9 6.1 %copy-start.2 = (bf16[128,2048]{1,0:T(8,128)(2,1)S(1)}, bf16[128,2048]{1,0:T(8,128)(2,1)}, u32[]{:S(2)}) copy-start(bf16[128,2048]{1,0:T(8,128)(2,1)} %act.1) | copy-start | bytes 1572868
  10.7 1.3 %copy-start.1 = (bf16[2,2048,256]{2,1,0:T(8,128)(2,1)}, bf16[2,2048,256]{2,1,0:T(8,128)(2,1)S(1)}, u32[]{:S(2)}) copy-start(bf16[2,2048,256]{2,1,0:T(8,128)(2,1)S(1)} %get-tuple-element.10.w_down) | copy-start | bytes 6291460

commit v2 on v1

--- a/solution.py
+++ b/solution.py
@@ -58,34 +58,6 @@
         for term in (own, received)
     )
     return (own_sum + other_sum).astype(jnp.bfloat16)
-
-
-def pick_kernel(lists, col, gate, up, down, gate_out, up_out, down_out):
-    gate_out[0] = gate[...]
-    up_out[0] = up[...]
-    down_out[0] = down[...]
-
-
-def pick(block_lists, col_id, w_gate, w_up, w_down):
-    depth, slab = w_gate.shape
-    blocks = block_lists.shape[0]
-    top = slab // WIDTH - 1
-
-    def chosen(b, s, lists, col):
-        return 0, jnp.minimum(lists[b, col[0], s], top)
-
-    shape = jax.ShapeDtypeStruct((blocks, depth, 2 * WIDTH), w_gate.dtype)
-    return pl.pallas_call(
-        pick_kernel,
-        grid_spec=pltpu.PrefetchScalarGridSpec(
-            num_scalar_prefetch=2,
-            grid=(blocks, 2),
-            in_specs=[pl.BlockSpec((depth, WIDTH), chosen)] * 3,
-            out_specs=[pl.BlockSpec((1, depth, WIDTH), lambda b, s, lists, col: (b, 0, s))] * 3,
-        ),
-        out_shape=[shape] * 3,
-        compiler_params=pltpu.CompilerParams(vmem_limit_bytes=32 * 2**20),
-    )(block_lists, col_id, w_gate, w_up, w_down)
 
 
 def layer_kernel(
@@ -104,13 +76,13 @@
     c2 = (c + 2) % 4
     c3 = (c1 + 2) % 4
 
-    loads = [
-        pltpu.make_async_copy(w_gate, gate_w, w_sem.at[0]),
-        pltpu.make_async_copy(w_up, up_w, w_sem.at[1]),
-        pltpu.make_async_copy(w_down, down_w, w_sem.at[2]),
-    ]
-    for load in loads:
-        load.start()
+    def load(source, target, sem):
+        for block in range(slab_blocks + 1):
+            at = min(block, slab_blocks - 1) * WIDTH
+            pltpu.make_async_copy(source.at[:, pl.ds(at, WIDTH)], target.at[block], sem).start()
+
+    def loaded(target, sem):
+        pltpu.make_async_copy(target, target, sem).wait()
 
     barrier = pltpu.get_barrier_semaphore()
     for dr in range(rows):
@@ -184,8 +156,10 @@
     def gate_up(p):
         for b in range(blocks):
             x = x_all[p, 2 * b : 2 * b + 2].reshape(2 * toks, depth)
-            for j, weight in enumerate((gate_w, up_w)):
-                value = jnp.dot(x, weight[b], preferred_element_type=jnp.float32)
+            for j in range(2):
+                block = lists[b, c, j]
+                weight = jnp.concatenate([gate_w[block], up_w[block]], axis=1)
+                value = jnp.dot(x, weight, preferred_element_type=jnp.float32)
                 value = value.reshape(2, toks, 2 * WIDTH)
                 lanes = slice(j * 2 * WIDTH, (j + 1) * 2 * WIDTH)
                 part_f32[p, 2 * b : 2 * b + 2, :, lanes] = value
@@ -199,11 +173,11 @@
         for k in range(1, rows):
             arrived(part_in.at[p, k - 1], p_recv.at[p, k])
             total = total + part_in[p, k - 1].astype(jnp.float32)
-        value = jnp.maximum(total[:, : 2 * WIDTH], 0.0) * total[:, 2 * WIDTH :]
-        live = [jnp.where(lists[r // 2, c, s] < slab_blocks, 1.0, 0.0) for s in range(2)]
-        lane = lax.broadcasted_iota(jnp.int32, value.shape, 1)
-        value = value * jnp.where(lane < WIDTH, live[0], live[1])
-        hid_all[p, r] = value.astype(jnp.bfloat16)
+        for j in range(2):
+            at = 2 * j * WIDTH
+            live = jnp.where(lists[r // 2, c, j] < slab_blocks, 1.0, 0.0)
+            value = jnp.maximum(total[:, at : at + WIDTH], 0.0) * total[:, at + WIDTH : at + 2 * WIDTH]
+            hid_all[p, r, :, j * WIDTH : (j + 1) * WIDTH] = (value * live).astype(jnp.bfloat16)
         for k in range(1, rows):
             mine = hid_all.at[p, r]
             send_to(mine, mine, h_send.at[p, k], h_recv.at[p, k], (r + k) % rows, c)
@@ -215,8 +189,11 @@
         for b in range(blocks):
             h = hid_all[p, 2 * b : 2 * b + 2].reshape(2 * toks, 2 * WIDTH)
             for n in range(0, depth, tile):
+                weight = jnp.concatenate(
+                    [down_w[lists[b, c, j], n : n + tile] for j in range(2)], axis=1
+                )
                 value = lax.dot_general(
-                    h, down_w[b, n : n + tile], (((1,), (1,)), ((), ())),
+                    h, weight, (((1,), (1,)), ((), ())),
                     preferred_element_type=jnp.float32,
                 ).astype(jnp.bfloat16)
                 for i in range(2):
@@ -249,18 +226,21 @@
 
     for p in range(parts):
         spread(p)
+    load(w_gate, gate_w, w_sem.at[0])
+    load(w_up, up_w, w_sem.at[1])
+    load(w_down, down_w, w_sem.at[2])
     forward(0)
     forward_again(0)
     forward(1)
     collected(0)
-    loads[0].wait()
-    loads[1].wait()
+    loaded(gate_w, w_sem.at[0])
+    loaded(up_w, w_sem.at[1])
     gate_up(0)
     forward_again(1)
     collected(1)
     gate_up(1)
     hidden(0)
-    loads[2].wait()
+    loaded(down_w, w_sem.at[2])
     down(0)
     hidden(1)
     pair(0)
@@ -284,6 +264,7 @@
     toks = cols * size
     bf16, f32 = jnp.bfloat16, jnp.float32
     sem = pltpu.SemaphoreType.DMA
+    slab = pltpu.VMEM((slab_blocks + 1, gate.shape[0], WIDTH), bf16)
     by_row, by_col = sem((PARTS, rows)), sem((PARTS, cols))
     return pl.pallas_call(
         functools.partial(layer_kernel, slab_blocks),
@@ -291,9 +272,7 @@
         in_specs=[pl.BlockSpec(memory_space=pltpu.SMEM)] + [pl.BlockSpec(memory_space=pl.ANY)] * 4,
         out_specs=pl.BlockSpec(memory_space=pltpu.VMEM),
         scratch_shapes=[
-            pltpu.VMEM(gate.shape, bf16),
-            pltpu.VMEM(up.shape, bf16),
-            pltpu.VMEM(down.shape, bf16),
+            slab, slab, slab,
             pltpu.VMEM((PARTS, rows, cols, size, depth), bf16),
             pltpu.VMEM((PARTS, rows, toks, 4 * WIDTH), f32),
             pltpu.VMEM((PARTS, rows, toks, 4 * WIDTH), bf16),
@@ -312,16 +291,14 @@
             by_row, by_row, by_row, by_col,
         ],
         compiler_params=pltpu.CompilerParams(
-            collective_id=0, has_side_effects=True, vmem_limit_bytes=48 * 2**20
+            collective_id=0, has_side_effects=True, vmem_limit_bytes=60 * 2**20
         ),
     )(block_lists, activations, gate, up, down)
 
 
 def near_shards(rows, cols, activations, w_gate, w_up, w_down, block_lists):
     slab_blocks = w_gate.shape[1] // WIDTH
-    col_id = lax.axis_index("col").astype(jnp.int32).reshape(1)
-    gate, up, down = pick(block_lists, col_id, w_gate, w_up, w_down)
-    return layer(block_lists, activations, gate, up, down, rows, cols, slab_blocks)
+    return layer(block_lists, activations, w_gate, w_up, w_down, rows, cols, slab_blocks)
 
 
 def solution(mesh):

time: 90 us -> 81.2 us (0.902)
  local copies, waits for them, and re-layouts: 8.07 us -> 3.24 us
  Pallas kernels: 81.7 us -> 77.7 us
    unnamed x8 -> x2, local copies, waits for them, and re-layouts: 8.07 us -> 3.24 us
    pallas_call x1 -> x0, Pallas kernels: 4.73 us -> none  [pick(): pl.pallas_call(pick_kernel, grid_spec=pltpu.PrefetchScalarGridSpec(num_sc...]
where the time goes in v2:
time: 81.2 us; the launch traced here: 81 us
  Pallas kernels  77.7 us (96%)
  local copies, waits for them, and re-layouts  3.24 us (4%)
    pallas_call x1, Pallas kernels, layer(): pl.pallas_call(functools.partial(layer_kernel, slab_blocks), out_shape=ja...  77.7 us
    unnamed x2, local copies, waits for them, and re-layouts  3.24 us

profile of v2, /device:TPU:1, one launch (start us, length us, event | category | flops | bytes accessed | tf_op | source)
XLA Modules:
  0.0 81.0 jit_solution(1231730940285177419)
XLA Ops:
  0.0 1.4 %copy.6.lists = s32[2,4,2]{2,1,0:T(4,128)} copy(s32[2,4,2]{1,2,0:T(2,128)} %param.9) | data formatting | bytes 128 | tf_op args[4]
  1.4 77.7 %shard_map.55 = bf16[128,2048]{1,0:T(8,128)(2,1)} custom-call(s32[2,4,2]{2,1,0:T(4,128)} %copy.6.lists, bf16[128,2048]{1,0:T(8,128)(2,1)} %act.1, bf16[2048,3584]{1,0:T(8,128)(2,1)} %w_gate.1, bf16[2048,3584]{1,0:T(8,128)(2,1)} %w_up.1, bf16[2048,3584]{1,0:T(8,128)(2,1)} %w_down.1), custom_call_target="tpu_custom_call" | custom-call | tf_op jit(solution)/shard_map/pallas_call | solution.py:269
  79.1 1.9 %copy.8 = bf16[128,2048]{1,0:T(8,128)(2,1)} copy(bf16[128,2048]{1,0:T(8,128)(2,1)} %shard_map.55) | data formatting | bytes 1048576

commit v3 on v2

--- a/solution.py
+++ b/solution.py
@@ -62,9 +62,9 @@
 
 def layer_kernel(
     slab_blocks, lists, act, w_gate, w_up, w_down, out,
-    gate_w, up_w, down_w, x_all, part_f32, part_out, part_in, hid_all,
+    gate_w, up_w, down_w, x_cross, x_all, part_f32, part_out, part_in, hid_all,
     term, term_in, half_out, half_in, sum_out,
-    w_sem, a_send, a_recv, g1_send, g1_recv, g2_send, g2_recv, g3_send, g3_recv,
+    w_sem, c_send, c_recv, a_send, a_recv, g1_send, g1_recv, g2_send, g2_recv, g3_send, g3_recv,
     p_send, p_recv, h_send, h_recv, t_send, t_recv, s_send, s_recv, o_send, o_recv,
 ):
     parts, rows, cols, size, depth = x_all.shape
@@ -125,11 +125,25 @@
     def arrived(dst, recv):
         pltpu.make_async_copy(dst, dst, recv).wait()
 
-    def spread(p):
-        for q in range(cols):
+    def cross(p):
+        at = (p * cols + 2 * (1 - chip)) * size
+        send_to(act.at[pl.ds(at, 2 * size)], x_cross.at[p], c_send.at[p], c_recv.at[p], r, c2)
+
+    def spread_own(p):
+        for j in range(2):
+            q = 2 * chip + j
             send_or_keep(
                 act.at[pl.ds((p * cols + q) * size, size)], x_all.at[p, r, q],
-                a_send.at[p, q], a_recv.at[p, r], c, q,
+                a_send.at[p, j], a_recv.at[p, r], c, q,
+            )
+
+    def spread_other(p):
+        arrived(x_cross.at[p], c_recv.at[p])
+        for j in range(2):
+            q = 2 * chip + j
+            send_or_keep(
+                x_cross.at[p, pl.ds(j * size, size)], x_all.at[p, r, q],
+                a_send.at[p, 2 + j], a_recv.at[p, r], c2, q,
             )
 
     def forward(p):
@@ -225,28 +239,31 @@
             )
 
     for p in range(parts):
-        spread(p)
+        cross(p)
+        spread_own(p)
     load(w_gate, gate_w, w_sem.at[0])
     load(w_up, up_w, w_sem.at[1])
     load(w_down, down_w, w_sem.at[2])
+    spread_other(0)
+    spread_other(1)
     forward(0)
+    forward(1)
     forward_again(0)
-    forward(1)
     collected(0)
     loaded(gate_w, w_sem.at[0])
     loaded(up_w, w_sem.at[1])
+    loaded(down_w, w_sem.at[2])
     gate_up(0)
     forward_again(1)
     collected(1)
     gate_up(1)
     hidden(0)
-    loaded(down_w, w_sem.at[2])
+    hidden(1)
     down(0)
-    hidden(1)
     pair(0)
     down(1)
+    pair(1)
     finish(0)
-    pair(1)
     finish(1)
     for p in range(parts):
         for q in range(cols):
@@ -273,6 +290,7 @@
         out_specs=pl.BlockSpec(memory_space=pltpu.VMEM),
         scratch_shapes=[
             slab, slab, slab,
+            pltpu.VMEM((PARTS, 2 * size, depth), bf16),
             pltpu.VMEM((PARTS, rows, cols, size, depth), bf16),
             pltpu.VMEM((PARTS, rows, toks, 4 * WIDTH), f32),
             pltpu.VMEM((PARTS, rows, toks, 4 * WIDTH), bf16),
@@ -284,6 +302,7 @@
             pltpu.VMEM((PARTS, rows, size, depth), bf16),
             pltpu.VMEM((PARTS, rows, size, depth), bf16),
             sem((3,)),
+            sem((PARTS,)), sem((PARTS,)),
             by_col, by_row,
             by_row, by_row, by_row, by_row, by_row, by_row,
             by_row, by_row, by_row, by_row,

time: 81.2 us -> 70.7 us (0.87)
  Pallas kernels: 77.7 us -> 67.3 us
    pallas_call x1, Pallas kernels: 77.7 us -> 67.3 us  [layer(): pl.pallas_call(functools.partial(layer_kernel, slab_blocks), out_shape=ja...]
where the time goes in v3:
time: 70.7 us; the launch traced here: 70.5 us
  Pallas kernels  67.3 us (95%)
  local copies, waits for them, and re-layouts  3.24 us (5%)
    pallas_call x1, Pallas kernels, layer(): pl.pallas_call(functools.partial(layer_kernel, slab_blocks), out_shape=ja...  67.3 us
    unnamed x2, local copies, waits for them, and re-layouts  3.24 us

profile of v3, /device:TPU:1, one launch (start us, length us, event | category | flops | bytes accessed | tf_op | source)
XLA Modules:
  0.0 70.5 jit_solution(9158217200260191753)
XLA Ops:
  0.0 1.4 %copy.6.lists = s32[2,4,2]{2,1,0:T(4,128)} copy(s32[2,4,2]{1,2,0:T(2,128)} %param.9) | data formatting | bytes 128 | tf_op args[4]
  1.4 67.3 %shard_map.55 = bf16[128,2048]{1,0:T(8,128)(2,1)} custom-call(s32[2,4,2]{2,1,0:T(4,128)} %copy.6.lists, bf16[128,2048]{1,0:T(8,128)(2,1)} %act.1, bf16[2048,3584]{1,0:T(8,128)(2,1)} %w_gate.1, bf16[2048,3584]{1,0:T(8,128)(2,1)} %w_up.1, bf16[2048,3584]{1,0:T(8,128)(2,1)} %w_down.1), custom_call_target="tpu_custom_call" | custom-call | tf_op jit(solution)/shard_map/pallas_call | solution.py:286
  68.7 1.9 %copy.8 = bf16[128,2048]{1,0:T(8,128)(2,1)} copy(bf16[128,2048]{1,0:T(8,128)(2,1)} %shard_map.55) | data formatting | bytes 1048576

commit v4 on v3

--- a/solution.py
+++ b/solution.py
@@ -178,15 +178,19 @@
                 lanes = slice(j * 2 * WIDTH, (j + 1) * 2 * WIDTH)
                 part_f32[p, 2 * b : 2 * b + 2, :, lanes] = value
                 part_out[p, 2 * b : 2 * b + 2, :, lanes] = value.astype(jnp.bfloat16)
-        for k in range(1, rows):
-            s = (r + k) % rows
-            send_to(part_out.at[p, s], part_in.at[p, k - 1], p_send.at[p, k], p_recv.at[p, k], s, c)
+            for s in (2 * b, 2 * b + 1):
+                k = (s - r + rows) % rows
+                copy = remote(
+                    part_out.at[p, s], part_in.at[p, k], p_send.at[p, s], p_recv.at[p, k], s, c
+                )
+                pl.when(s != r)(copy.start)
+                drains.append((s != r, copy))
 
     def hidden(p):
         total = part_f32[p, r]
         for k in range(1, rows):
-            arrived(part_in.at[p, k - 1], p_recv.at[p, k])
-            total = total + part_in[p, k - 1].astype(jnp.float32)
+            arrived(part_in.at[p, k], p_recv.at[p, k])
+            total = total + part_in[p, k].astype(jnp.float32)
         for j in range(2):
             at = 2 * j * WIDTH
             live = jnp.where(lists[r // 2, c, j] < slab_blocks, 1.0, 0.0)
@@ -238,25 +242,26 @@
                 o_send.at[p, k], o_recv.at[p, c], s, r,
             )
 
-    for p in range(parts):
-        cross(p)
-        spread_own(p)
+    cross(0)
+    spread_own(0)
+    cross(1)
+    spread_other(0)
+    spread_own(1)
     load(w_gate, gate_w, w_sem.at[0])
     load(w_up, up_w, w_sem.at[1])
     load(w_down, down_w, w_sem.at[2])
-    spread_other(0)
+    forward(0)
     spread_other(1)
-    forward(0)
+    forward_again(0)
     forward(1)
-    forward_again(0)
     collected(0)
     loaded(gate_w, w_sem.at[0])
     loaded(up_w, w_sem.at[1])
-    loaded(down_w, w_sem.at[2])
     gate_up(0)
     forward_again(1)
     collected(1)
     gate_up(1)
+    loaded(down_w, w_sem.at[2])
     hidden(0)
     hidden(1)
     down(0)
@@ -294,7 +299,7 @@
             pltpu.VMEM((PARTS, rows, cols, size, depth), bf16),
             pltpu.VMEM((PARTS, rows, toks, 4 * WIDTH), f32),
             pltpu.VMEM((PARTS, rows, toks, 4 * WIDTH), bf16),
-            pltpu.VMEM((PARTS, rows - 1, toks, 4 * WIDTH), bf16),
+            pltpu.VMEM((PARTS, rows, toks, 4 * WIDTH), bf16),
             pltpu.VMEM((PARTS, rows, toks, 2 * WIDTH), bf16),
             pltpu.VMEM((PARTS, 2, 2, rows, size, depth), bf16),
             pltpu.VMEM((PARTS, 2, rows, size, depth), bf16),

time: 70.7 us -> 70.5 us (level)
  no operation moved by 1% of the time
where the time goes in v4:
time: 70.5 us; the launch traced here: 70.3 us
  Pallas kernels  67 us (95%)
  local copies, waits for them, and re-layouts  3.24 us (5%)
    pallas_call x1, Pallas kernels, layer(): pl.pallas_call(functools.partial(layer_kernel, slab_blocks), out_shape=ja...  67 us
    unnamed x2, local copies, waits for them, and re-layouts  3.24 us

profile of v4, /device:TPU:1, one launch (start us, length us, event | category | flops | bytes accessed | tf_op | source)
XLA Modules:
  0.0 70.3 jit_solution(5404763954654655626)
XLA Ops:
  0.0 1.4 %copy.6.lists = s32[2,4,2]{2,1,0:T(4,128)} copy(s32[2,4,2]{1,2,0:T(2,128)} %param.9) | data formatting | bytes 128 | tf_op args[4]
  1.4 67.0 %shard_map.55 = bf16[128,2048]{1,0:T(8,128)(2,1)} custom-call(s32[2,4,2]{2,1,0:T(4,128)} %copy.6.lists, bf16[128,2048]{1,0:T(8,128)(2,1)} %act.1, bf16[2048,3584]{1,0:T(8,128)(2,1)} %w_gate.1, bf16[2048,3584]{1,0:T(8,128)(2,1)} %w_up.1, bf16[2048,3584]{1,0:T(8,128)(2,1)} %w_down.1), custom_call_target="tpu_custom_call" | custom-call | tf_op jit(solution)/shard_map/pallas_call | solution.py:291
  68.4 1.9 %copy.8 = bf16[128,2048]{1,0:T(8,128)(2,1)} copy(bf16[128,2048]{1,0:T(8,128)(2,1)} %shard_map.55) | data formatting | bytes 1048576
